TPU v7x, 32 devices: a whole 2x2x4 slice. The times are simulated.
32 devices in a mesh: lat: 8 (over z, x), lev: 4 (over y, core).
Axes of the slice: x: 2, y: 2, z: 4, core: 2. Of those that a mesh axis runs over, the one named last changes fastest.
Arguments:
- particle_mass_fraction: float32 [20, 64, 8, 360], P(None, 'lat', 'lev'), may hold values from 0.1 to 2
- meridional_cfl_factor: float32 [64, 8, 360], P('lat', 'lev'), may hold values from -0.45 to 0.45
- thermal_state_kelvins: float32 [64, 8, 360], P('lat', 'lev'), may hold values from 200 to 300
- logarithmic_barometric_span: float32 [8], P('lev'), may hold values from 0.06 to 0.2
- gravitational_fall_kilometres: float32 [20], replicated, may hold values from 0.02 to 20
- zonal_cfl_factor: float32 [64, 8, 360], P('lat', None, 'lev'), may hold values from -0.45 to 0.45
- collision_rate_matrix: float32 [20, 20], replicated, may hold values from 0.02 to 0.2
Outputs:
- dust_out: float32 [20, 64, 8, 360], P(None, 'lat', None, 'lev')
- height: float32 [64, 8, 360], P('lat', 'lev')
All inputs are finite; a program needn't handle non-finite values.
Results may differ from a plain program's by a relative error of at most 0.000067.
Values sent between devices are 32-bit elements; how exact they have to be, the bound alone decides.
A program may use at most 128 MiB of HBM per device.

v0:
```python
import functools

import jax
import jax.numpy as jnp
from jax import lax
from jax.experimental import pallas as pl
from jax.experimental.pallas import tpu as pltpu
from jax.sharding import PartitionSpec as P

specific_air_factor = 0.0293
scale_height = 7.0
LANES = 128
MESH = pl.DeviceIdType.MESH
HIGHEST = lax.Precision.HIGHEST


def widen(x):
    short = -x.shape[-1] % LANES
    if short:
        x = jnp.concatenate([x, jnp.zeros((*x.shape[:-1], short), x.dtype)], -1)
    return x


def lon_block(tile, total, width, block):
    axis = 2
    count = -(-total // LANES)
    last = total % LANES
    start = block * width - 1
    c, off = start // LANES, start % LANES

    def piece(i):
        if i < 0:
            return pltpu.roll(tile(count - 1), (LANES - last) % LANES, axis)
        if i == count:
            return tile(0)
        x = tile(i)
        if i == count - 1 and last and total < start + width + 2:
            lane = lax.broadcasted_iota(jnp.int32, x.shape, axis)
            x = jnp.where(lane < last, x, pltpu.roll(tile(0), last, axis))
        return x

    x = piece(c)
    if off + width + 2 > LANES:
        lane = lax.broadcasted_iota(jnp.int32, x.shape, axis)
        x = jnp.where(lane >= off, x, piece(c + 1))
    return pltpu.roll(x, (2 * LANES - off - 1) % LANES, axis)


def spare(lane, width):
    return (lane > width) & (lane < LANES - 1)


def stow(x, d, width, p):
    free = LANES - 2 - width
    lane = lax.broadcasted_iota(jnp.int32, x.shape, 2)
    return jnp.where(spare(lane, width), pltpu.roll(d, (width + 2 - p * free) % LANES, 2), x)


def unstow(parts, width):
    free = LANES - 2 - width
    back = [pltpu.roll(x, (p * free - width - 2) % LANES, 2) for p, x in enumerate(parts)]
    lane = lax.broadcasted_iota(jnp.int32, back[0].shape, 2)
    later = jnp.where(lane < 2 * free - 1, back[1], back[2])
    return jnp.where((lane < free - 1) | (lane == LANES - 1), back[0], later)


def kernel(
    n_lat, n_lev,
    q_hbm, mc_hbm, temp_hbm, span_hbm, fall_hbm, zc_hbm, rate_hbm,
    out_ref, height_ref,
    q_ref, mc_ref, temp_ref, span_ref, fall_ref, zc_ref, rate_ref,
    main_s, main_r, thick_s, thick_r, north_s, north_r, south_s, south_r,
    tot_s, tot_r, zc_s, zc_r, inverse, advected, kron, dens,
    main_ss, main_rs, thick_ss, thick_rs, north_ss, north_rs, south_ss, south_rs,
    tot_ss, tot_rs, zc_sem, own_sem, load_sem,
):
    i, j = lax.axis_index("lat"), lax.axis_index("lev")
    loads = [
        pltpu.make_async_copy(src, dst, load_sem.at[number])
        for number, (src, dst) in enumerate((
            (span_hbm, span_ref), (temp_hbm, temp_ref), (zc_hbm, zc_ref), (mc_hbm, mc_ref),
            (q_hbm, q_ref), (fall_hbm, fall_ref), (rate_hbm, rate_ref)))
    ]
    for load in loads:
        load.start()
    bins, rows, levels, total = q_ref.shape
    width = total // n_lev
    left, right = lax.rem(j + n_lev - 1, n_lev), lax.rem(j + 1, n_lev)
    has_south, has_north = i > 0, i < n_lat - 1

    barrier = pltpu.get_barrier_semaphore()
    for d in range(1, n_lev):
        pl.semaphore_signal(barrier, inc=1, device_id=(i, lax.rem(j + d, n_lev)), device_id_type=MESH)

    @pl.when(has_south)
    def _():
        for m in range(n_lev):
            pl.semaphore_signal(barrier, inc=1, device_id=(i - 1, m), device_id_type=MESH)

    @pl.when(has_north)
    def _():
        for m in range(n_lev):
            pl.semaphore_signal(barrier, inc=1, device_id=(i + 1, m), device_id_type=MESH)

    for load in loads[:3]:
        load.wait()
    thick = [specific_air_factor * temp_ref[:, k, :] * span_ref[k] for k in range(levels)]
    tot = thick[0]
    for k in range(1, levels):
        tot = tot + thick[k]
    tot_s[...] = widen(tot)
    for m in range(n_lev):
        for k in range(levels):
            wide = widen(thick[k])[None]
            tile = lambda c: wide[:, :, c * LANES : (c + 1) * LANES]
            thick_s[m, k] = lon_block(tile, total, width, m)[0]
    zc_s[...] = widen(zc_ref[...])

    peers = n_lev - 1 + n_lev * (jnp.minimum(i, 1) + jnp.minimum(n_lat - 1 - i, 1))

    def thick_copy(m):
        return pltpu.make_async_remote_copy(
            thick_s.at[m], thick_r.at[j], thick_ss.at[m], thick_rs.at[j], (i, m), MESH)

    def main_copy(m):
        return pltpu.make_async_remote_copy(
            main_s.at[m], main_r.at[j], main_ss.at[m], main_rs.at[j], (i, m), MESH)

    def tot_copy(m):
        return pltpu.make_async_remote_copy(
            tot_s, tot_r.at[j], tot_ss.at[m], tot_rs.at[j], (i, m), MESH)

    def north_copy(m):
        return pltpu.make_async_remote_copy(
            north_s.at[m], north_r.at[j], north_ss.at[m], north_rs.at[j], (i + 1, m), MESH)

    def south_copy(m):
        return pltpu.make_async_remote_copy(
            south_s.at[m], south_r.at[j], south_ss.at[m], south_rs.at[j], (i - 1, m), MESH)

    zc_copy = pltpu.make_async_remote_copy(
        zc_s, zc_r, zc_sem.at[0], zc_sem.at[1], (i, left), MESH)

    def tile_of(ref, k):
        def tile(c):
            stop = min((c + 1) * LANES, total)
            return widen(ref[:, :, k, c * LANES : stop])
        return tile

    def mc_tile(k):
        def tile(c):
            stop = min((c + 1) * LANES, total)
            return widen(mc_ref[:, k, c * LANES : stop])[None]
        return tile

    for load in loads[3:5]:
        load.wait()
    group = bins // 4

    def cut_block(m):
        for k in range(levels):
            x = lon_block(tile_of(q_ref, k), total, width, m)
            for p in range(3):
                main_s[m, k, pl.ds(p * group, group)] = stow(
                    x[p * group : (p + 1) * group], x[3 * group :], width, p)
            main_s[m, k, pl.ds(3 * group, 1)] = lon_block(mc_tile(k), total, width, m)
            south_s[m, k] = main_s[m, k, :, 0, :]
            north_s[m, k] = main_s[m, k, :, rows - 1, :]

    def send_edges(m):
        @pl.when(has_south)
        def _():
            south_copy(m).start()

        @pl.when(has_north)
        def _():
            north_copy(m).start()

    half_way = n_lev // 2
    base = half_way * (j // half_way)

    def cut_half(first):
        for m in range(first, first + half_way):
            cut_block(m)

    @pl.when(j >= half_way)
    def _():
        cut_half(0)

    @pl.when(j < half_way)
    def _():
        cut_half(half_way)

    pl.semaphore_wait(barrier, peers)

    for m in range(n_lev):
        @pl.when(j != m)
        def _():
            thick_copy(m).start()
    for s in range(half_way):
        main_copy(half_way - base + s).start()
    for s in range(half_way):
        send_edges(half_way - base + s)
    zc_copy.start()

    @pl.when(j >= half_way)
    def _():
        cut_half(half_way)

    @pl.when(j < half_way)
    def _():
        cut_half(0)

    for s in range(half_way):
        m = base + s

        @pl.when(j != m)
        def _():
            main_copy(m).start()
        send_edges(m)

    for m in range(n_lev):
        @pl.when(j > m)
        def _():
            tot_copy(m).start()

    own = [pltpu.make_async_copy(main_s.at[j], main_r.at[j], own_sem.at[0]),
           pltpu.make_async_copy(thick_s.at[j], thick_r.at[j], own_sem.at[1])]
    for copy in own:
        copy.start()

    @pl.when(jnp.logical_not(has_south))
    def _():
        north_r[...] = jnp.zeros_like(north_r)

    @pl.when(jnp.logical_not(has_north))
    def _():
        south_r[...] = jnp.zeros_like(south_r)

    for load in loads[5:]:
        load.wait()
    rate = rate_ref[...]
    r0 = lax.broadcasted_iota(jnp.int32, rate.shape, 0)
    r1 = lax.broadcasted_iota(jnp.int32, rate.shape, 1)
    merging = jnp.where(r1 < r0, rate, jnp.where(r1 > r0, -rate, 0.0))
    cells = bins * rows
    e0 = lax.broadcasted_iota(jnp.int32, (cells, bins), 0)
    e1 = lax.broadcasted_iota(jnp.int32, (cells, bins), 1)
    spread = jnp.where((e0 >= e1 * rows) & (e0 < (e1 + 1) * rows), 1.0, 0.0)
    half = jnp.dot(spread, merging, precision=HIGHEST, preferred_element_type=jnp.float32)
    full = lax.dot_general(half, spread, (((1,), (1,)), ((), ())), precision=HIGHEST,
                           preferred_element_type=jnp.float32)
    k0 = lax.broadcasted_iota(jnp.int32, full.shape, 0)
    k1 = lax.broadcasted_iota(jnp.int32, full.shape, 1)
    kron[...] = jnp.where(lax.rem(k0, rows) == lax.rem(k1, rows), full, 0.0)

    own[1].wait()
    for m in range(n_lev):
        @pl.when(j != m)
        def _():
            pltpu.make_async_remote_copy(
                thick_s.at[m], thick_r.at[m], thick_ss.at[m], thick_rs.at[m], (i, m), MESH).wait_recv()
    below = jnp.zeros((rows, LANES), jnp.float32)
    for k in reversed(range(n_lev * levels)):
        t = thick_r[k // levels, k % levels]
        dens[k] = jnp.exp((below + 0.5 * t) * (-1.0 / scale_height))
        below = below + t
        for b in range(bins):
            inverse[k, b] = 1.0 / (t + fall_ref[b])

    own[0].wait()

    sub = lax.broadcasted_iota(jnp.int32, (1, rows, LANES), 1)
    lane = lax.broadcasted_iota(jnp.int32, (1, rows, LANES), 2)
    for s in range(n_lev):
        m = lax.rem(base + s, n_lev)

        @pl.when(j != m)
        def _():
            pltpu.make_async_remote_copy(
                main_s.at[m], main_r.at[m], main_ss.at[m], main_rs.at[m], (i, m), MESH).wait_recv()

        @pl.when(has_south)
        def _():
            pltpu.make_async_remote_copy(
                north_s.at[m], north_r.at[m], north_ss.at[m], north_rs.at[m], (i - 1, m), MESH).wait_recv()

        @pl.when(has_north)
        def _():
            pltpu.make_async_remote_copy(
                south_s.at[m], south_r.at[m], south_ss.at[m], south_rs.at[m], (i + 1, m), MESH).wait_recv()

        for kk in range(levels):
            q = main_r[m, kk, pl.ds(0, 3 * group)].reshape(3, group, rows, LANES)
            mc = main_r[m, kk, pl.ds(3 * group, 1)]
            q_below = north_r[m, kk, pl.ds(0, 3 * group)].reshape(3, group, 1, LANES)
            q_above = south_r[m, kk, pl.ds(0, 3 * group)].reshape(3, group, 1, LANES)
            mc_above = south_r[m, kk, pl.ds(3 * group, 1)][:, None, :]
            mc_n = jnp.where(sub == rows - 1, mc_above, pltpu.roll(mc, rows - 1, 1))
            parts = []
            for p in range(3):
                c_s, c_n = stow(mc, mc, width, p), stow(mc_n, mc_n, width, p)
                x = q[p]
                q_s = jnp.where(sub == 0, q_below[p], pltpu.roll(x, 1, 1))
                q_n = jnp.where(sub == rows - 1, q_above[p], pltpu.roll(x, rows - 1, 1))
                south = jnp.maximum(c_s, 0.0) * q_s + jnp.minimum(c_s, 0.0) * x
                north = jnp.maximum(c_n, 0.0) * x + jnp.minimum(c_n, 0.0) * q_n
                parts.append(x + south - north)
            parts.append(unstow(parts, width))
            for p in range(4):
                advected[m * levels + kk, pl.ds(p * group, group)] = parts[p]

    zc_copy.wait_recv()
    flow = jnp.zeros((bins, rows, LANES), jnp.float32)
    for k in range(n_lev * levels):
        t = thick_r[k // levels, pl.ds(k % levels, 1)]
        summed = advected[k] + flow
        settled = (t * inverse[k]) * summed
        flow = summed - settled
        z = jnp.where(lane == width, pltpu.roll(zc_r[:, k, :][None], width, 2), zc_s[:, k, :][None])
        west = jnp.maximum(z, 0.0) * pltpu.roll(settled, 1, 2) + jnp.minimum(z, 0.0) * settled
        moved = settled + west - pltpu.roll(west, LANES - 1, 2)
        coag = jnp.dot(kron[...], moved.reshape(cells, LANES), precision=HIGHEST,
                       preferred_element_type=jnp.float32).reshape(moved.shape)
        result = moved + dens[pl.ds(k, 1)] * moved * coag
        out_ref[:, :, k, :] = result[:, :, :width]

    below = jnp.zeros((rows, total), jnp.float32)
    for m in range(n_lev):
        @pl.when(j >= m)
        def _():
            tot_r[m] = jnp.zeros_like(tot_s)

        @pl.when(j < m)
        def _():
            pltpu.make_async_remote_copy(
                tot_s, tot_r.at[m], tot_ss.at[m], tot_rs.at[m], (i, m), MESH).wait_recv()

        below = below + tot_r[m][:, :total]
    for k in reversed(range(levels)):
        t = specific_air_factor * temp_ref[:, k, :] * span_ref[k]
        height_ref[:, k, :] = below + 0.5 * t
        below = below + t

    zc_copy.wait_send()
    for m in range(n_lev):
        @pl.when(j != m)
        def _():
            thick_copy(m).wait_send()
            main_copy(m).wait_send()

        @pl.when(j > m)
        def _():
            tot_copy(m).wait_send()

        @pl.when(has_south)
        def _():
            south_copy(m).wait_send()

        @pl.when(has_north)
        def _():
            north_copy(m).wait_send()


def hand_over(dust_ref, height_ref, dust_out, height_out, sem_out):
    pieces = sem_out.shape[0] - 1
    step = dust_ref.shape[0] // pieces
    leave = [pltpu.make_async_copy(height_ref, height_out, sem_out.at[pieces])]
    for p in range(pieces):
        part = pl.ds(p * step, step)
        leave.append(pltpu.make_async_copy(dust_ref.at[part], dust_out.at[part], sem_out.at[p]))
    for copy in leave:
        copy.start()
    for copy in leave:
        copy.wait()


def solution(mesh):
    n_lat, n_lev = mesh.shape["lat"], mesh.shape["lev"]
    vmem = pl.BlockSpec(memory_space=pltpu.VMEM)
    hbm = pl.BlockSpec(memory_space=pltpu.HBM)

    def on_device(q, mc, temp, span, fall, zc, rate):
        bins, rows, levels, total = q.shape
        width = total // n_lev
        assert width + 2 <= 3 * (LANES - 2 - width) and bins % 4 == 0
        packed = 3 * bins // 4 + 1
        deep = n_lev * levels
        wide = -(-total // LANES) * LANES
        f32 = jnp.float32
        main = pltpu.VMEM((n_lev, levels, packed, rows, LANES), f32)
        thick = pltpu.VMEM((n_lev, levels, rows, LANES), f32)
        edge = pltpu.VMEM((n_lev, levels, packed, LANES), f32)
        zonal = pltpu.VMEM((rows, deep, LANES), f32)
        sems = pltpu.SemaphoreType.DMA((n_lev,))
        pair = pltpu.SemaphoreType.DMA((2,))
        q, mc, temp, span, fall, zc, rate = (
            pltpu.with_memory_space_constraint(x, pltpu.HBM) for x in (q, mc, temp, span, fall, zc, rate))
        dust, height = pl.pallas_call(
            functools.partial(kernel, n_lat, n_lev),
            out_shape=(
                pltpu.VMEM((bins, rows, deep, width), f32),
                pltpu.VMEM((rows, levels, total), f32),
            ),
            in_specs=[hbm] * 7,
            out_specs=(vmem, vmem),
            scratch_shapes=[
                pltpu.VMEM(q.shape, f32), pltpu.VMEM(mc.shape, f32), pltpu.VMEM(temp.shape, f32),
                pltpu.SMEM(span.shape, f32), pltpu.SMEM(fall.shape, f32),
                pltpu.VMEM(zc.shape, f32), pltpu.VMEM(rate.shape, f32),
                main, main, thick, thick, edge, edge, edge, edge,
                pltpu.VMEM((rows, wide), f32), pltpu.VMEM((n_lev, rows, wide), f32),
                zonal, zonal,
                pltpu.VMEM((deep, bins, rows, LANES), f32),
                pltpu.VMEM((deep, bins, rows, LANES), f32),
                pltpu.VMEM((bins * rows, bins * rows), f32),
                pltpu.VMEM((deep, rows, LANES), f32),
            ] + [sems] * 10 + [pair] * 2 + [pltpu.SemaphoreType.DMA((7,))],
            compiler_params=pltpu.CompilerParams(
                collective_id=0, has_side_effects=True, vmem_limit_bytes=24 * 1024 * 1024),
        )(q, mc, temp, span, fall, zc, rate)
        return pl.pallas_call(
            hand_over,
            out_shape=(
                jax.ShapeDtypeStruct(dust.shape, f32), jax.ShapeDtypeStruct(height.shape, f32)),
            in_specs=[vmem, vmem],
            out_specs=(hbm, hbm),
            scratch_shapes=[pltpu.SemaphoreType.DMA((5,))],
            compiler_params=pltpu.CompilerParams(vmem_limit_bytes=24 * 1024 * 1024),
        )(dust, height)

    in_specs = (
        P(None, "lat", "lev", None),
        P("lat", "lev", None),
        P("lat", "lev", None),
        P("lev"),
        P(),
        P("lat", None, "lev"),
        P(),
    )
    out_specs = (P(None, "lat", None, "lev"), P("lat", "lev", None))
    return jax.shard_map(
        on_device, mesh=mesh, in_specs=in_specs, out_specs=out_specs, check_vma=False
    )
```

profile of v0, /device:TPU:1, one launch (start us, length us, event | category | flops | bytes accessed | tf_op | source)
XLA Modules:
  0.0 15.8 jit_solution(6977365377611396374)
XLA Ops:
  0.6 14.3 %shard_map.86 = (f32[20,8,8,90]{3,2,1,0:T(8,128)S(1)}, f32[8,2,360]{2,1,0:T(2,128)S(1)}) custom-call(f32[20,8,2,360]{3,2,1,0:T(2,128)} %q_hbm.1, f32[8,2,360]{2,1,0:T(2,128)} %mc_hbm.1, f32[8,2,360]{2,1,0:T(2,128)} %temp_hbm.1, f32[2]{0:T(128)} %span_hbm.1, f32[20]{0:T(128)} %fall_hbm.1, f32[8,8,90]{2,1,0:T(8,128)} %zc_hbm.1, f32[20,20]{1,0:T(8,128)} %rate_hbm.1), custom_call_target="tpu_custom_call" | custom-call | tf_op jit(solution)/shard_map/pallas_call | solution.py:399
  14.9 0.9 %shard_map.87 = (f32[20,8,8,90]{3,2,1,0:T(8,128)}, f32[8,2,360]{2,1,0:T(2,128)}) custom-call(f32[20,8,8,90]{3,2,1,0:T(8,128)S(1)} %get-tuple-element.4.dust_ref, f32[8,2,360]{2,1,0:T(2,128)S(1)} %get-tuple-element.5.height_ref), custom_call_target="tpu_custom_call" | custom-call | tf_op jit(solution)/shard_map/pallas_call | solution.py:422
where the time goes:
time: 15.9 us; the launch traced here: 15.8 us
  Pallas kernels  15.2 us (96%)
  between operations  0.64 us (4%)
    pallas_call x1, Pallas kernels, on_device(): pl.pallas_call(functools.partial(kernel, n_lat, n_lev), out_shape=(pltpu....  14.3 us
    pallas_call x1, Pallas kernels, on_device(): pl.pallas_call(hand_over, out_shape=(jax.ShapeDtypeStruct(dust.shape, f32...  0.88 us

commit v1 on v0

v1 whole, which is shorter than its diff:
```python
import functools

import jax
import jax.numpy as jnp
from jax import lax
from jax.experimental import pallas as pl
from jax.experimental.pallas import tpu as pltpu
from jax.sharding import PartitionSpec as P

specific_air_factor = 0.0293
scale_height = 7.0
LANES = 128
TILE = 8
MESH = pl.DeviceIdType.MESH
HIGHEST = lax.Precision.HIGHEST


def widen(x):
    short = -x.shape[-1] % LANES
    if short:
        x = jnp.concatenate([x, jnp.zeros((*x.shape[:-1], short), x.dtype)], -1)
    return x


def lon_block(tile, total, width, block):
    count = -(-total // LANES)
    last = total % LANES
    start = block * width - 1
    c, off = start // LANES, start % LANES

    def piece(i):
        if i < 0:
            x = tile(count - 1)
            return pltpu.roll(x, (LANES - last) % LANES, x.ndim - 1)
        if i == count:
            return tile(0)
        x = tile(i)
        if i == count - 1 and last and total < start + width + 2:
            lane = lax.broadcasted_iota(jnp.int32, x.shape, x.ndim - 1)
            x = jnp.where(lane < last, x, pltpu.roll(tile(0), last, x.ndim - 1))
        return x

    x = piece(c)
    if off + width + 2 > LANES:
        lane = lax.broadcasted_iota(jnp.int32, x.shape, x.ndim - 1)
        x = jnp.where(lane >= off, x, piece(c + 1))
    return pltpu.roll(x, (2 * LANES - off - 1) % LANES, x.ndim - 1)


def row_pairs(rows):
    return [(r, r + 1) for r in range(1, rows - 1, 2)] + [(0, rows - 1)]


def kernel(
    n_lat, n_lev,
    q_hbm, mc_hbm, temp_hbm, span_hbm, fall_hbm, zc_hbm, rate_hbm,
    out_ref, height_ref,
    q_v, mc_v, temp_v, span_s, fall_s, zc_v, rate_v,
    main_s, main_r, thick_s, thick_r, south_r, north_r, mcn_r, below_s, below_r,
    halo_s, halo_r, adv_v, ratio_v, dens_v, z_v, merge_v,
    q_sem, load_sem, main_ss, main_rs, thick_ss, thick_rs,
    below_ss, below_rs, north_ss, north_rs, south_ss, south_rs, halo_sem,
):
    i, j = lax.axis_index("lat"), lax.axis_index("lev")
    rows, levels, bins, total = q_v.shape
    width = total // n_lev
    full = bins // TILE
    rest = bins % TILE
    body = full * TILE
    pairs = row_pairs(rows)
    stack = 2 * bins
    carriers = 2 * full
    deep = n_lev * levels
    piece = -(-(width + 2) // carriers)
    padded = -(-stack // 16) * 16
    count = -(-total // LANES)
    half_way = n_lev // 2
    has_south, has_north = i > 0, i < n_lat - 1
    left = lax.rem(j + n_lev - 1, n_lev)

    barrier = pltpu.get_barrier_semaphore()
    for d in range(1, n_lev):
        pl.semaphore_signal(barrier, inc=1, device_id=(i, lax.rem(j + d, n_lev)), device_id_type=MESH)

    @pl.when(has_south)
    def _():
        pl.semaphore_signal(barrier, inc=1, device_id=(i - 1, j), device_id_type=MESH)

    @pl.when(has_north)
    def _():
        pl.semaphore_signal(barrier, inc=1, device_id=(i + 1, j), device_id_type=MESH)

    small = [
        pltpu.make_async_copy(src, dst, load_sem.at[number])
        for number, (src, dst) in enumerate((
            (span_hbm, span_s), (temp_hbm, temp_v), (mc_hbm, mc_v), (zc_hbm, zc_v),
            (fall_hbm, fall_s), (rate_hbm, rate_v)))
    ]
    big = [[pltpu.make_async_copy(q_hbm.at[:, r, k, :], q_v.at[r, k], q_sem.at[r * levels + k])
            for k in range(levels)] for r in range(rows)]
    for load in small[:4]:
        load.start()
    order = list(dict.fromkeys(
        n for pair in pairs for r in pair for n in (r - 1, r, r + 1) if 0 <= n < rows))
    for r in order:
        for load in big[r]:
            load.start()
    for load in small[4:]:
        load.start()

    def main_copy(m, ch):
        return pltpu.make_async_remote_copy(
            main_s.at[m, ch], main_r.at[j, ch], main_ss.at[m, ch], main_rs.at[j, ch], (i, m), MESH)

    def main_arrival(m, ch):
        return pltpu.make_async_remote_copy(
            main_s.at[m, ch], main_r.at[m, ch], main_ss.at[m, ch], main_rs.at[m, ch], (i, m), MESH)

    def thick_copy(m):
        return pltpu.make_async_remote_copy(
            thick_s.at[m], thick_r.at[j], thick_ss.at[m], thick_rs.at[j], (i, m), MESH)

    def below_copy(m):
        return pltpu.make_async_remote_copy(
            below_s.at[m], below_r.at[j], below_ss.at[m], below_rs.at[j], (i, m), MESH)

    north_copies = [
        pltpu.make_async_remote_copy(
            q_hbm.at[:, rows - 1, k, :], south_r.at[k], north_ss.at[k], north_rs.at[k], (i + 1, j), MESH)
        for k in range(levels)]
    south_copies = [
        pltpu.make_async_remote_copy(
            q_hbm.at[:, 0, k, :], north_r.at[k], south_ss.at[k], south_rs.at[k], (i - 1, j), MESH)
        for k in range(levels)]
    south_copies.append(pltpu.make_async_remote_copy(
        mc_hbm.at[0], mcn_r, south_ss.at[levels], south_rs.at[levels], (i - 1, j), MESH))
    halo_copy = pltpu.make_async_remote_copy(
        halo_s, halo_r, halo_sem.at[0], halo_sem.at[1], (i, left), MESH)

    lane = lax.broadcasted_iota(jnp.int32, (TILE, LANES), 1)
    sub = lax.broadcasted_iota(jnp.int32, (TILE, LANES), 0)
    spare = (lane > width) & (lane <= width + piece)
    zlane = lax.broadcasted_iota(jnp.int32, (deep, LANES), 1)
    base = half_way * (j // half_way)
    far = [half_way - base + n for n in range(half_way)]
    near = [base + lax.rem(j - base + n, half_way) for n in range(1, half_way)]
    waited = set()

    def lanes_of(c):
        return slice(c * LANES, min((c + 1) * LANES, total))

    def prepare(ch):
        for r in order:
            if r not in waited and any(abs(r - r2) < 2 for r2 in pairs[ch]):
                waited.add(r)
                for load in big[r]:
                    load.wait()
        for k in range(levels):
            for c in range(count):
                at = lanes_of(c)
                for side, r in enumerate(pairs[ch]):
                    x = widen(q_v[r, k, :, at])
                    south = widen(q_v[r - 1, k, :, at] if r > 0 else south_r[k, :, at])
                    north = widen(q_v[r + 1, k, :, at] if r < rows - 1 else north_r[k, :, at])
                    c_s = widen(mc_v[r, k : k + 1, at])
                    c_n = widen(mc_v[r + 1, k : k + 1, at] if r < rows - 1 else mcn_r[k : k + 1, at])
                    keep = 1.0 + jnp.minimum(c_s, 0.0) - jnp.maximum(c_n, 0.0)
                    x = keep * x + jnp.maximum(c_s, 0.0) * south - jnp.minimum(c_n, 0.0) * north
                    adv_v[ch, k, c, side * body : (side + 1) * body] = x[:body]
                    low = 2 * body + side * rest
                    adv_v[ch, k, c, low : low + rest] = x[body:]
        for m in range(n_lev):
            for k in range(levels):
                x = lon_block(lambda c: adv_v[ch, k, c], total, width, m)
                extra = x[2 * body :]
                for p in range(carriers):
                    at = slice(p * TILE, (p + 1) * TILE)
                    main_s[m, ch, k, at] = jnp.where(
                        spare, pltpu.roll(extra, (width + 2 - piece * p) % LANES, 1), x[at])

    def send(ch):
        for m in far + near:
            main_copy(m, ch).start()
        main_r[pl.ds(j, 1), ch] = main_s[pl.ds(j, 1), ch]

    for load in small[:4]:
        load.wait()
    for k in range(levels):
        wide = widen(specific_air_factor * temp_v[:, k, :] * span_s[k])
        tile = lambda c: wide[:, c * LANES : (c + 1) * LANES]
        for m in range(n_lev):
            thick_s[m, k] = lon_block(tile, total, width, m)
    zc = widen(zc_v[...])
    halo = jnp.zeros((deep, LANES), jnp.float32)
    for r in range(rows):
        halo = jnp.where(zlane == r, pltpu.roll(zc[r], r, 1) if r else zc[r], halo)
        z_v[r] = zc[r]
    halo_s[...] = halo
    prepare(0)

    pl.semaphore_wait(barrier, n_lev - 1 + jnp.minimum(i, 1) + jnp.minimum(n_lat - 1 - i, 1))
    for m in far:
        thick_copy(m).start()
    for m in far:
        main_copy(m, 0).start()

    @pl.when(has_north)
    def _():
        for copy in north_copies:
            copy.start()

    @pl.when(has_south)
    def _():
        for copy in south_copies:
            copy.start()

    halo_copy.start()
    for m in near:
        thick_copy(m).start()
    for m in near:
        main_copy(m, 0).start()
    main_r[pl.ds(j, 1), 0] = main_s[pl.ds(j, 1), 0]
    thick_r[pl.ds(j, 1)] = thick_s[pl.ds(j, 1)]

    prepare(1)
    send(1)

    for load in small[4:]:
        load.wait()
    rate = rate_v[...]
    r0 = lax.broadcasted_iota(jnp.int32, rate.shape, 0)
    r1 = lax.broadcasted_iota(jnp.int32, rate.shape, 1)
    merging = jnp.where(r1 < r0, rate, jnp.where(r1 > r0, -rate, 0.0))

    def place(n):
        tail = n - 2 * body
        side = jnp.where(n < 2 * body, n // body, tail // rest)
        kind = jnp.where(n < 2 * body, n - side * body, body + tail - side * rest)
        return side, jnp.where(n < stack, kind, -1)

    _, kind = place(lax.broadcasted_iota(jnp.int32, (padded, bins), 0))
    pick = jnp.where(kind == lax.broadcasted_iota(jnp.int32, (padded, bins), 1), 1.0, 0.0)
    both = jnp.dot(pick, merging, precision=HIGHEST, preferred_element_type=jnp.float32)
    both = lax.dot_general(both, pick, (((1,), (1,)), ((), ())), precision=HIGHEST,
                           preferred_element_type=jnp.float32)
    side0, _ = place(lax.broadcasted_iota(jnp.int32, (padded, padded), 0))
    side1, _ = place(lax.broadcasted_iota(jnp.int32, (padded, padded), 1))
    both = jnp.where(side0 == side1, both, 0.0)
    high = both.astype(jnp.bfloat16)
    low = (both - high.astype(jnp.float32)).astype(jnp.bfloat16)
    merge_v[...] = jnp.concatenate([high, high, low], 1)

    def column(first, n):
        x = jnp.zeros((TILE, LANES), jnp.float32)
        for s in range(TILE):
            x = jnp.where(sub == s, fall_s[first + s % n], x)
        return x

    fall = [column(f * TILE, TILE) for f in range(full)]
    fall = jnp.concatenate(fall + fall + [column(body, rest)], 0)

    def spread(a, b):
        return jnp.concatenate([
            jnp.broadcast_to(a, (body, LANES)), jnp.broadcast_to(b, (body, LANES)),
            jnp.where(sub < rest, a, b)], 0)

    prepare(2)
    send(2)
    for ch in range(3, len(pairs) - 1):
        prepare(ch)
        send(ch)

    for m in range(n_lev):
        @pl.when(j != m)
        def _():
            pltpu.make_async_remote_copy(
                thick_s.at[m], thick_r.at[m], thick_ss.at[m], thick_rs.at[m], (i, m), MESH).wait_recv()
    below = jnp.zeros((rows, LANES), jnp.float32)
    for m in reversed(range(n_lev)):
        below_s[m] = below
        for k in reversed(range(levels)):
            t = thick_r[m, k]
            dens_v[m * levels + k] = jnp.exp((below + 0.5 * t) * (-1.0 / scale_height))
            below = below + t
    for m in far + near:
        below_copy(m).start()
    below_r[pl.ds(j, 1)] = below_s[pl.ds(j, 1)]

    for ch, (r, r2) in enumerate(pairs):
        for k in range(deep):
            t = spread(thick_r[k // levels, k % levels, r : r + 1], thick_r[k // levels, k % levels, r2 : r2 + 1])
            ratio_v[ch, k] = t / (t + fall)

    halo_copy.wait_recv()
    halo = halo_r[...]
    for r in range(rows):
        z_v[r] = jnp.where(zlane == width, pltpu.roll(halo, width - r, 1), z_v[r])

    def collect(ch):
        r, r2 = pairs[ch]
        flow = jnp.zeros((stack, LANES), jnp.float32)
        for group in range(0, n_lev, 2):
            for m in (group, group + 1):
                @pl.when(j != m)
                def _():
                    main_arrival(m, ch).wait_recv()

            moved = []
            ks = range(group * levels, (group + 2) * levels)
            for k in ks:
                x = main_r[k // levels, ch, k % levels]
                extra = None
                for p in reversed(range(carriers)):
                    part = pltpu.roll(x[p * TILE : (p + 1) * TILE], (piece * p - width - 2) % LANES, 1)
                    if extra is None:
                        extra = part
                    else:
                        first = lane < piece * (p + 1) - 1
                        extra = jnp.where(first | (lane == LANES - 1) if p == 0 else first, part, extra)
                x = jnp.concatenate([x, extra], 0)
                summed = x + flow
                settled = ratio_v[ch, k] * summed
                flow = summed - settled
                z, z2 = z_v[r, k : k + 1], z_v[r2, k : k + 1]
                up = spread(jnp.maximum(z, 0.0), jnp.maximum(z2, 0.0))
                down = spread(jnp.minimum(z, 0.0), jnp.minimum(z2, 0.0))
                west = up * pltpu.roll(settled, 1, 1) + down * settled
                moved.append(settled + west - pltpu.roll(west, LANES - 1, 1))
            x = jnp.concatenate(moved, 1)
            x = jnp.concatenate([x, jnp.zeros((padded - stack, x.shape[1]), jnp.float32)], 0)
            high = x.astype(jnp.bfloat16)
            low = (x - high.astype(jnp.float32)).astype(jnp.bfloat16)
            coag = jnp.dot(merge_v[...], jnp.concatenate([high, low, high], 0),
                           preferred_element_type=jnp.float32)
            for n, k in enumerate(ks):
                dens = spread(dens_v[k, r : r + 1], dens_v[k, r2 : r2 + 1])
                x = moved[n]
                x = (x + dens * x * coag[:stack, n * LANES : (n + 1) * LANES])[:, :width]
                out_ref[r, k, :body] = x[:body]
                out_ref[r2, k, :body] = x[body : 2 * body]
                out_ref[r, k, body:] = x[2 * body : 2 * body + rest]
                out_ref[r2, k, body:] = x[2 * body + rest :]

    @pl.when(jnp.logical_not(has_south))
    def _():
        south_r[...] = jnp.zeros_like(south_r)

    @pl.when(jnp.logical_not(has_north))
    def _():
        north_r[...] = jnp.zeros_like(north_r)
        mcn_r[...] = jnp.zeros_like(mcn_r)

    @pl.when(has_south)
    def _():
        for k in range(levels):
            pltpu.make_async_remote_copy(
                q_hbm.at[:, 0, k, :], south_r.at[k], north_ss.at[k], north_rs.at[k], (i - 1, j), MESH).wait_recv()

    @pl.when(has_north)
    def _():
        for k in range(levels):
            pltpu.make_async_remote_copy(
                q_hbm.at[:, 0, k, :], north_r.at[k], south_ss.at[k], south_rs.at[k], (i + 1, j), MESH).wait_recv()
        pltpu.make_async_remote_copy(
            mc_hbm.at[0], mcn_r, south_ss.at[levels], south_rs.at[levels], (i + 1, j), MESH).wait_recv()

    final = len(pairs) - 1
    prepare(final)
    send(final)
    for ch in range(final):
        collect(ch)

    for m in range(n_lev):
        @pl.when(j != m)
        def _():
            pltpu.make_async_remote_copy(
                below_s.at[m], below_r.at[m], below_ss.at[m], below_rs.at[m], (i, m), MESH).wait_recv()
    lower = []
    for c in range(count):
        x = jnp.zeros((rows, LANES), jnp.float32)
        for m in range(n_lev):
            first, end = m * width - c * LANES, (m + 1) * width - c * LANES
            if first < LANES and end > 0:
                x = jnp.where((lane >= first) & (lane < end), pltpu.roll(below_r[m], first % LANES, 1), x)
        lower.append(x)
    below = jnp.concatenate(lower, 1)[:, :total]
    for k in reversed(range(levels)):
        t = specific_air_factor * temp_v[:, k, :] * span_s[k]
        height_ref[:, k, :] = below + 0.5 * t
        below = below + t

    halo_copy.wait_send()
    for m in far + near:
        thick_copy(m).wait_send()
        below_copy(m).wait_send()
        for ch in range(final):
            main_copy(m, ch).wait_send()

    @pl.when(has_south)
    def _():
        for copy in south_copies:
            copy.wait_send()

    @pl.when(has_north)
    def _():
        for copy in north_copies:
            copy.wait_send()

    collect(final)
    for m in far + near:
        main_copy(m, final).wait_send()


def hand_over(dust_ref, height_ref, dust_out, height_out, sem_out):
    rows, deep = dust_ref.shape[:2]
    leave = [pltpu.make_async_copy(height_ref, height_out, sem_out.at[rows * deep])]
    for r in range(rows):
        for k in range(deep):
            leave.append(pltpu.make_async_copy(
                dust_ref.at[r, k], dust_out.at[:, r, k, :], sem_out.at[r * deep + k]))
    for copy in leave:
        copy.start()
    for copy in leave:
        copy.wait()


def solution(mesh):
    n_lat, n_lev = mesh.shape["lat"], mesh.shape["lev"]
    vmem = pl.BlockSpec(memory_space=pltpu.VMEM)
    hbm = pl.BlockSpec(memory_space=pltpu.HBM)

    def on_device(*args):
        bins, rows, levels, total = args[0].shape
        width = total // n_lev
        full, rest = bins // 8, bins % 8
        carriers = 2 * full
        piece = -(-(width + 2) // carriers)
        assert rest == 4 and rows == 8 and width + 1 + piece < LANES and n_lev % 2 == 0
        deep = n_lev * levels
        count = -(-total // LANES)
        chunks = len(row_pairs(rows))
        stack = 2 * bins
        padded = -(-stack // 16) * 16
        f32 = jnp.float32
        main = pltpu.VMEM((n_lev, chunks, levels, carriers * TILE, LANES), f32)
        thick = pltpu.VMEM((n_lev, levels, rows, LANES), f32)
        edge = pltpu.VMEM((levels, bins, total), f32)
        tile = pltpu.VMEM((n_lev, rows, LANES), f32)
        halo = pltpu.VMEM((deep, LANES), f32)
        dma = pltpu.SemaphoreType.DMA
        args = [pltpu.with_memory_space_constraint(x, pltpu.HBM) for x in args]
        dust, height = pl.pallas_call(
            functools.partial(kernel, n_lat, n_lev),
            out_shape=(
                pltpu.VMEM((rows, deep, bins, width), f32),
                pltpu.VMEM((rows, levels, total), f32),
            ),
            in_specs=[hbm] * 7,
            out_specs=(vmem, vmem),
            scratch_shapes=[
                pltpu.VMEM((rows, levels, bins, total), f32),
                pltpu.VMEM((rows, levels, total), f32), pltpu.VMEM((rows, levels, total), f32),
                pltpu.SMEM((levels,), f32), pltpu.SMEM((bins,), f32),
                pltpu.VMEM((rows, deep, width), f32), pltpu.VMEM((bins, bins), f32),
                main, main, thick, thick, edge, edge, pltpu.VMEM((levels, total), f32), tile, tile,
                halo, halo,
                pltpu.VMEM((chunks, levels, count, stack, LANES), f32),
                pltpu.VMEM((chunks, deep, stack, LANES), f32),
                pltpu.VMEM((deep, rows, LANES), f32),
                pltpu.VMEM((rows, deep, LANES), f32),
                                pltpu.VMEM((padded, 3 * padded), jnp.bfloat16),
                dma((rows * levels,)), dma((6,)),
                dma((n_lev, chunks)), dma((n_lev, chunks)),
                dma((n_lev,)), dma((n_lev,)), dma((n_lev,)), dma((n_lev,)),
                dma((levels,)), dma((levels,)), dma((levels + 1,)), dma((levels + 1,)), dma((2,)),
            ],
            compiler_params=pltpu.CompilerParams(
                collective_id=0, has_side_effects=True, vmem_limit_bytes=32 * 1024 * 1024),
        )(*args)
        return pl.pallas_call(
            hand_over,
            out_shape=(
                jax.ShapeDtypeStruct((bins, rows, deep, width), f32),
                jax.ShapeDtypeStruct(height.shape, f32)),
            in_specs=[vmem, vmem],
            out_specs=(hbm, hbm),
            scratch_shapes=[dma((rows * deep + 1,))],
            compiler_params=pltpu.CompilerParams(vmem_limit_bytes=32 * 1024 * 1024),
        )(dust, height)

    in_specs = (
        P(None, "lat", "lev", None),
        P("lat", "lev", None),
        P("lat", "lev", None),
        P("lev"),
        P(),
        P("lat", None, "lev"),
        P(),
    )
    out_specs = (P(None, "lat", None, "lev"), P("lat", "lev", None))
    return jax.shard_map(
        on_device, mesh=mesh, in_specs=in_specs, out_specs=out_specs, check_vma=False
    )
```

time: 15.9 us -> 14.1 us (0.89)
  the two profiles are of different devices: /device:TPU:1 before, /device:TPU:0 now
where the time goes in v1:
time: 14.1 us; the launch traced here: 13.9 us
  Pallas kernels  13.3 us (94%)
  between operations  0.64 us (5%)
    pallas_call x1, Pallas kernels, on_device(): pl.pallas_call(functools.partial(kernel, n_lat, n_lev), out_shape=(pltpu....  11.9 us
    pallas_call x1, Pallas kernels, on_device(): pl.pallas_call(hand_over, out_shape=(jax.ShapeDtypeStruct((bins, rows, de...  1.42 us

profile of v1, /device:TPU:0, one launch (start us, length us, event | category | flops | bytes accessed | tf_op | source)
XLA Modules:
  0.0 13.9 jit_solution(10947304051599370181)
XLA Ops:
  0.6 11.9 %shard_map.86 = (f32[8,8,20,90]{3,2,1,0:T(8,128)S(1)}, f32[8,2,360]{2,1,0:T(2,128)S(1)}) custom-call(f32[20,8,2,360]{3,2,1,0:T(2,128)} %q_hbm.1, f32[8,2,360]{2,1,0:T(2,128)} %mc_hbm.1, f32[8,2,360]{2,1,0:T(2,128)} %temp_hbm.1, f32[2]{0:T(128)} %span_hbm.1, f32[20]{0:T(128)} %fall_hbm.1, f32[8,8,90]{2,1,0:T(8,128)} %zc_hbm.1, f32[20,20]{1,0:T(8,128)} %rate_hbm.1), custom_call_target="tpu_custom_call" | custom-call | tf_op jit(solution)/shard_map/pallas_call | solution.py:452
  12.5 1.4 %shard_map.87 = (f32[20,8,8,90]{3,2,1,0:T(8,128)}, f32[8,2,360]{2,1,0:T(2,128)}) custom-call(f32[8,8,20,90]{3,2,1,0:T(8,128)S(1)} %get-tuple-element.4.dust_ref, f32[8,2,360]{2,1,0:T(2,128)S(1)} %get-tuple-element.5.height_ref), custom_call_target="tpu_custom_call" | custom-call | tf_op jit(solution)/shard_map/pallas_call | solution.py:480

commit v2 on v1

--- a/solution.py
+++ b/solution.py
@@ -336,10 +336,10 @@
                 dens = spread(dens_v[k, r : r + 1], dens_v[k, r2 : r2 + 1])
                 x = moved[n]
                 x = (x + dens * x * coag[:stack, n * LANES : (n + 1) * LANES])[:, :width]
-                out_ref[r, k, :body] = x[:body]
-                out_ref[r2, k, :body] = x[body : 2 * body]
-                out_ref[r, k, body:] = x[2 * body : 2 * body + rest]
-                out_ref[r2, k, body:] = x[2 * body + rest :]
+                out_ref[:body, r, k, :] = x[:body]
+                out_ref[:body, r2, k, :] = x[body : 2 * body]
+                out_ref[body:, r, k, :] = x[2 * body : 2 * body + rest]
+                out_ref[body:, r2, k, :] = x[2 * body + rest :]
 
     @pl.when(jnp.logical_not(has_south))
     def _():
@@ -412,12 +412,13 @@
 
 
 def hand_over(dust_ref, height_ref, dust_out, height_out, sem_out):
-    rows, deep = dust_ref.shape[:2]
-    leave = [pltpu.make_async_copy(height_ref, height_out, sem_out.at[rows * deep])]
-    for r in range(rows):
-        for k in range(deep):
-            leave.append(pltpu.make_async_copy(
-                dust_ref.at[r, k], dust_out.at[:, r, k, :], sem_out.at[r * deep + k]))
+    pieces = sem_out.shape[0] - 1
+    step = dust_ref.shape[0] // pieces
+    leave = []
+    for p in range(pieces):
+        part = pl.ds(p * step, step)
+        leave.append(pltpu.make_async_copy(dust_ref.at[part], dust_out.at[part], sem_out.at[p]))
+    leave.append(pltpu.make_async_copy(height_ref, height_out, sem_out.at[pieces]))
     for copy in leave:
         copy.start()
     for copy in leave:
@@ -452,7 +453,7 @@
         dust, height = pl.pallas_call(
             functools.partial(kernel, n_lat, n_lev),
             out_shape=(
-                pltpu.VMEM((rows, deep, bins, width), f32),
+                pltpu.VMEM((bins, rows, deep, width), f32),
                 pltpu.VMEM((rows, levels, total), f32),
             ),
             in_specs=[hbm] * 7,
@@ -484,7 +485,7 @@
                 jax.ShapeDtypeStruct(height.shape, f32)),
             in_specs=[vmem, vmem],
             out_specs=(hbm, hbm),
-            scratch_shapes=[dma((rows * deep + 1,))],
+            scratch_shapes=[dma((5,))],
             compiler_params=pltpu.CompilerParams(vmem_limit_bytes=32 * 1024 * 1024),
         )(dust, height)
 

time: 14.1 us -> 13.6 us (0.965)
  Pallas kernels: 13.3 us -> 12.8 us
    pallas_call x1, Pallas kernels: 1.42 us -> 0.88 us  [on_device(): pl.pallas_call(hand_over, out_shape=(jax.ShapeDtypeStruct((bins, rows, de...]
where the time goes in v2:
time: 13.6 us; the launch traced here: 13.4 us
  Pallas kernels  12.8 us (94%)
  between operations  0.64 us (5%)
    pallas_call x1, Pallas kernels, on_device(): pl.pallas_call(functools.partial(kernel, n_lat, n_lev), out_shape=(pltpu....  11.9 us
    pallas_call x1, Pallas kernels, on_device(): pl.pallas_call(hand_over, out_shape=(jax.ShapeDtypeStruct((bins, rows, de...  0.88 us

profile of v2, /device:TPU:0, one launch (start us, length us, event | category | flops | bytes accessed | tf_op | source)
XLA Modules:
  0.0 13.4 jit_solution(8933607232282617076)
XLA Ops:
  0.6 11.9 %shard_map.86 = (f32[20,8,8,90]{3,2,1,0:T(8,128)S(1)}, f32[8,2,360]{2,1,0:T(2,128)S(1)}) custom-call(f32[20,8,2,360]{3,2,1,0:T(2,128)} %q_hbm.1, f32[8,2,360]{2,1,0:T(2,128)} %mc_hbm.1, f32[8,2,360]{2,1,0:T(2,128)} %temp_hbm.1, f32[2]{0:T(128)} %span_hbm.1, f32[20]{0:T(128)} %fall_hbm.1, f32[8,8,90]{2,1,0:T(8,128)} %zc_hbm.1, f32[20,20]{1,0:T(8,128)} %rate_hbm.1), custom_call_target="tpu_custom_call" | custom-call | tf_op jit(solution)/shard_map/pallas_call | solution.py:453
  12.5 0.9 %shard_map.87 = (f32[20,8,8,90]{3,2,1,0:T(8,128)}, f32[8,2,360]{2,1,0:T(2,128)}) custom-call(f32[20,8,8,90]{3,2,1,0:T(8,128)S(1)} %get-tuple-element.4.dust_ref, f32[8,2,360]{2,1,0:T(2,128)S(1)} %get-tuple-element.5.height_ref), custom_call_target="tpu_custom_call" | custom-call | tf_op jit(solution)/shard_map/pallas_call | solution.py:481

commit v3 on v2

--- a/solution.py
+++ b/solution.py
@@ -57,7 +57,7 @@
     out_ref, height_ref,
     q_v, mc_v, temp_v, span_s, fall_s, zc_v, rate_v,
     main_s, main_r, thick_s, thick_r, south_r, north_r, mcn_r, below_s, below_r,
-    halo_s, halo_r, adv_v, ratio_v, dens_v, z_v, merge_v,
+    halo_s, halo_r, adv_v, ratio_v, dens_v, full_v, z_v, merge_v,
     q_sem, load_sem, main_ss, main_rs, thick_ss, thick_rs,
     below_ss, below_rs, north_ss, north_rs, south_ss, south_rs, halo_sem,
 ):
@@ -69,9 +69,9 @@
     body = full * TILE
     pairs = row_pairs(rows)
     stack = 2 * bins
-    carriers = 2 * full
     deep = n_lev * levels
-    piece = -(-(width + 2) // carriers)
+    piece = -(-(width + 2) // 3)
+    base_row, ends = 6 * TILE, slice(7 * TILE, 7 * TILE + TILE // 2)
     padded = -(-stack // 16) * 16
     count = -(-total // LANES)
     half_way = n_lev // 2
@@ -140,6 +140,29 @@
     lane = lax.broadcasted_iota(jnp.int32, (TILE, LANES), 1)
     sub = lax.broadcasted_iota(jnp.int32, (TILE, LANES), 0)
     spare = (lane > width) & (lane <= width + piece)
+    upper = sub < TILE // 2
+    first = (lane < piece - 1) | (lane == LANES - 1)
+    second = lane < 2 * piece - 1
+
+    def there(x, p):
+        return pltpu.roll(x, (width + 2 - piece * p) % LANES, 1)
+
+    def back(x, p):
+        return pltpu.roll(x, (piece * p - width - 2) % LANES, 1)
+
+    def twelve(a, b):
+        turned = pltpu.roll(b, TILE // 2, 0)
+        a = jnp.where(spare, jnp.where(upper, there(turned, 0), there(b, 1)), a)
+        return a, jnp.where(spare, there(turned, 2), b)[: TILE // 2]
+
+    def sixteen(a, b):
+        b = jnp.concatenate([b, b], 0)
+        outer = jnp.where(first, back(a, 0), back(b, 2))
+        inner = second & jnp.logical_not(first)
+        return a, jnp.where(upper, b, jnp.where(inner, back(a, 1), pltpu.roll(outer, TILE // 2, 0)))
+
+    def tiles(x):
+        return [x[n * TILE : (n + 1) * TILE] for n in range(x.shape[0] // TILE)]
     zlane = lax.broadcasted_iota(jnp.int32, (deep, LANES), 1)
     base = half_way * (j // half_way)
     far = [half_way - base + n for n in range(half_way)]
@@ -170,13 +193,11 @@
                     low = 2 * body + side * rest
                     adv_v[ch, k, c, low : low + rest] = x[body:]
         for m in range(n_lev):
-            for k in range(levels):
-                x = lon_block(lambda c: adv_v[ch, k, c], total, width, m)
-                extra = x[2 * body :]
-                for p in range(carriers):
-                    at = slice(p * TILE, (p + 1) * TILE)
-                    main_s[m, ch, k, at] = jnp.where(
-                        spare, pltpu.roll(extra, (width + 2 - piece * p) % LANES, 1), x[at])
+            x, y = (tiles(lon_block(lambda c: adv_v[ch, k, c], total, width, m)) for k in range(levels))
+            for n, carrier in enumerate(x[:4] + y[:2]):
+                main_s[m, ch, n * TILE : (n + 1) * TILE] = jnp.where(
+                    spare, there(y[2 + n // 3], n % 3), carrier)
+            main_s[m, ch, base_row : base_row + TILE], main_s[m, ch, ends] = twelve(x[4], y[4])
 
     def send(ch):
         for m in far + near:
@@ -185,11 +206,11 @@
 
     for load in small[:4]:
         load.wait()
-    for k in range(levels):
-        wide = widen(specific_air_factor * temp_v[:, k, :] * span_s[k])
-        tile = lambda c: wide[:, c * LANES : (c + 1) * LANES]
-        for m in range(n_lev):
-            thick_s[m, k] = lon_block(tile, total, width, m)
+    wide = [widen(specific_air_factor * temp_v[:, k, :] * span_s[k]) for k in range(levels)]
+    for m in range(n_lev):
+        x, y = (lon_block(lambda c: wide[k][:, c * LANES : (c + 1) * LANES], total, width, m)
+                for k in range(levels))
+        thick_s[m, :TILE], thick_s[m, TILE:] = twelve(x, y)
     zc = widen(zc_v[...])
     halo = jnp.zeros((deep, LANES), jnp.float32)
     for r in range(rows):
@@ -199,6 +220,11 @@
     prepare(0)
 
     pl.semaphore_wait(barrier, n_lev - 1 + jnp.minimum(i, 1) + jnp.minimum(n_lat - 1 - i, 1))
+    @pl.when(has_south)
+    def _():
+        for copy in south_copies:
+            copy.start()
+
     for m in far:
         thick_copy(m).start()
     for m in far:
@@ -207,11 +233,6 @@
     @pl.when(has_north)
     def _():
         for copy in north_copies:
-            copy.start()
-
-    @pl.when(has_south)
-    def _():
-        for copy in south_copies:
             copy.start()
 
     halo_copy.start()
@@ -224,6 +245,30 @@
 
     prepare(1)
     send(1)
+
+    prepare(2)
+    send(2)
+    for ch in range(3, len(pairs) - 1):
+        prepare(ch)
+        send(ch)
+
+    for m in range(n_lev):
+        @pl.when(j != m)
+        def _():
+            pltpu.make_async_remote_copy(
+                thick_s.at[m], thick_r.at[m], thick_ss.at[m], thick_rs.at[m], (i, m), MESH).wait_recv()
+    below = jnp.zeros((rows, LANES), jnp.float32)
+    for m in reversed(range(n_lev)):
+        below_s[m] = below
+        t2 = sixteen(thick_r[m, :TILE], thick_r[m, TILE:])
+        for k in reversed(range(levels)):
+            t = t2[k]
+            full_v[m * levels + k] = t
+            dens_v[m * levels + k] = jnp.exp((below + 0.5 * t) * (-1.0 / scale_height))
+            below = below + t
+    for m in far + near:
+        below_copy(m).start()
+    below_r[pl.ds(j, 1)] = below_s[pl.ds(j, 1)]
 
     for load in small[4:]:
         load.wait()
@@ -264,31 +309,35 @@
             jnp.broadcast_to(a, (body, LANES)), jnp.broadcast_to(b, (body, LANES)),
             jnp.where(sub < rest, a, b)], 0)
 
-    prepare(2)
-    send(2)
-    for ch in range(3, len(pairs) - 1):
-        prepare(ch)
-        send(ch)
-
-    for m in range(n_lev):
-        @pl.when(j != m)
-        def _():
+    @pl.when(jnp.logical_not(has_south))
+    def _():
+        south_r[...] = jnp.zeros_like(south_r)
+
+    @pl.when(jnp.logical_not(has_north))
+    def _():
+        north_r[...] = jnp.zeros_like(north_r)
+        mcn_r[...] = jnp.zeros_like(mcn_r)
+
+    @pl.when(has_south)
+    def _():
+        for k in range(levels):
             pltpu.make_async_remote_copy(
-                thick_s.at[m], thick_r.at[m], thick_ss.at[m], thick_rs.at[m], (i, m), MESH).wait_recv()
-    below = jnp.zeros((rows, LANES), jnp.float32)
-    for m in reversed(range(n_lev)):
-        below_s[m] = below
-        for k in reversed(range(levels)):
-            t = thick_r[m, k]
-            dens_v[m * levels + k] = jnp.exp((below + 0.5 * t) * (-1.0 / scale_height))
-            below = below + t
-    for m in far + near:
-        below_copy(m).start()
-    below_r[pl.ds(j, 1)] = below_s[pl.ds(j, 1)]
-
+                q_hbm.at[:, 0, k, :], south_r.at[k], north_ss.at[k], north_rs.at[k], (i - 1, j), MESH).wait_recv()
+
+    @pl.when(has_north)
+    def _():
+        for k in range(levels):
+            pltpu.make_async_remote_copy(
+                q_hbm.at[:, 0, k, :], north_r.at[k], south_ss.at[k], south_rs.at[k], (i + 1, j), MESH).wait_recv()
+        pltpu.make_async_remote_copy(
+            mc_hbm.at[0], mcn_r, south_ss.at[levels], south_rs.at[levels], (i + 1, j), MESH).wait_recv()
+
+    final = len(pairs) - 1
+    prepare(final)
+    send(final)
     for ch, (r, r2) in enumerate(pairs):
         for k in range(deep):
-            t = spread(thick_r[k // levels, k % levels, r : r + 1], thick_r[k // levels, k % levels, r2 : r2 + 1])
+            t = spread(full_v[k, r : r + 1], full_v[k, r2 : r2 + 1])
             ratio_v[ch, k] = t / (t + fall)
 
     halo_copy.wait_recv()
@@ -307,18 +356,15 @@
 
             moved = []
             ks = range(group * levels, (group + 2) * levels)
+            unpacked = []
+            for m in (group, group + 1):
+                x = tiles(main_r[m, ch, :base_row])
+                extra = [jnp.where(first, back(a, 0), jnp.where(second, back(b, 1), back(c, 2)))
+                         for a, b, c in (x[:3], x[3:])]
+                a, b = sixteen(main_r[m, ch, base_row : base_row + TILE], main_r[m, ch, ends])
+                unpacked += [x[:4] + [a], x[4:] + extra + [b]]
             for k in ks:
-                x = main_r[k // levels, ch, k % levels]
-                extra = None
-                for p in reversed(range(carriers)):
-                    part = pltpu.roll(x[p * TILE : (p + 1) * TILE], (piece * p - width - 2) % LANES, 1)
-                    if extra is None:
-                        extra = part
-                    else:
-                        first = lane < piece * (p + 1) - 1
-                        extra = jnp.where(first | (lane == LANES - 1) if p == 0 else first, part, extra)
-                x = jnp.concatenate([x, extra], 0)
-                summed = x + flow
+                summed = jnp.concatenate(unpacked[k - group * levels], 0) + flow
                 settled = ratio_v[ch, k] * summed
                 flow = summed - settled
                 z, z2 = z_v[r, k : k + 1], z_v[r2, k : k + 1]
@@ -341,32 +387,6 @@
                 out_ref[body:, r, k, :] = x[2 * body : 2 * body + rest]
                 out_ref[body:, r2, k, :] = x[2 * body + rest :]
 
-    @pl.when(jnp.logical_not(has_south))
-    def _():
-        south_r[...] = jnp.zeros_like(south_r)
-
-    @pl.when(jnp.logical_not(has_north))
-    def _():
-        north_r[...] = jnp.zeros_like(north_r)
-        mcn_r[...] = jnp.zeros_like(mcn_r)
-
-    @pl.when(has_south)
-    def _():
-        for k in range(levels):
-            pltpu.make_async_remote_copy(
-                q_hbm.at[:, 0, k, :], south_r.at[k], north_ss.at[k], north_rs.at[k], (i - 1, j), MESH).wait_recv()
-
-    @pl.when(has_north)
-    def _():
-        for k in range(levels):
-            pltpu.make_async_remote_copy(
-                q_hbm.at[:, 0, k, :], north_r.at[k], south_ss.at[k], south_rs.at[k], (i + 1, j), MESH).wait_recv()
-        pltpu.make_async_remote_copy(
-            mc_hbm.at[0], mcn_r, south_ss.at[levels], south_rs.at[levels], (i + 1, j), MESH).wait_recv()
-
-    final = len(pairs) - 1
-    prepare(final)
-    send(final)
     for ch in range(final):
         collect(ch)
 
@@ -379,9 +399,9 @@
     for c in range(count):
         x = jnp.zeros((rows, LANES), jnp.float32)
         for m in range(n_lev):
-            first, end = m * width - c * LANES, (m + 1) * width - c * LANES
-            if first < LANES and end > 0:
-                x = jnp.where((lane >= first) & (lane < end), pltpu.roll(below_r[m], first % LANES, 1), x)
+            begin, end = m * width - c * LANES, (m + 1) * width - c * LANES
+            if begin < LANES and end > 0:
+                x = jnp.where((lane >= begin) & (lane < end), pltpu.roll(below_r[m], begin % LANES, 1), x)
         lower.append(x)
     below = jnp.concatenate(lower, 1)[:, :total]
     for k in reversed(range(levels)):
@@ -434,17 +454,16 @@
         bins, rows, levels, total = args[0].shape
         width = total // n_lev
         full, rest = bins // 8, bins % 8
-        carriers = 2 * full
-        piece = -(-(width + 2) // carriers)
-        assert rest == 4 and rows == 8 and width + 1 + piece < LANES and n_lev % 2 == 0
+        assert full == 2 and rest == 4 and rows == 8 and levels == 2 and n_lev % 2 == 0
+        assert width + 1 + -(-(width + 2) // 3) < LANES
         deep = n_lev * levels
         count = -(-total // LANES)
         chunks = len(row_pairs(rows))
         stack = 2 * bins
         padded = -(-stack // 16) * 16
         f32 = jnp.float32
-        main = pltpu.VMEM((n_lev, chunks, levels, carriers * TILE, LANES), f32)
-        thick = pltpu.VMEM((n_lev, levels, rows, LANES), f32)
+        main = pltpu.VMEM((n_lev, chunks, 7 * TILE + TILE // 2, LANES), f32)
+        thick = pltpu.VMEM((n_lev, rows + TILE // 2, LANES), f32)
         edge = pltpu.VMEM((levels, bins, total), f32)
         tile = pltpu.VMEM((n_lev, rows, LANES), f32)
         halo = pltpu.VMEM((deep, LANES), f32)
@@ -467,7 +486,7 @@
                 halo, halo,
                 pltpu.VMEM((chunks, levels, count, stack, LANES), f32),
                 pltpu.VMEM((chunks, deep, stack, LANES), f32),
-                pltpu.VMEM((deep, rows, LANES), f32),
+                pltpu.VMEM((deep, rows, LANES), f32), pltpu.VMEM((deep, rows, LANES), f32),
                 pltpu.VMEM((rows, deep, LANES), f32),
                                 pltpu.VMEM((padded, 3 * padded), jnp.bfloat16),
                 dma((rows * levels,)), dma((6,)),

time: 13.6 us -> 13.5 us (level)
  Pallas kernels: 12.8 us -> 12.6 us
    pallas_call x1, Pallas kernels: 11.9 us -> 11.8 us  [on_device(): pl.pallas_call(functools.partial(kernel, n_lat, n_lev), out_shape=(pltpu....]
where the time goes in v3:
time: 13.5 us; the launch traced here: 13.3 us
  Pallas kernels  12.6 us (93%)
  between operations  0.64 us (5%)
    pallas_call x1, Pallas kernels, on_device(): pl.pallas_call(functools.partial(kernel, n_lat, n_lev), out_shape=(pltpu....  11.8 us
    pallas_call x1, Pallas kernels, on_device(): pl.pallas_call(hand_over, out_shape=(jax.ShapeDtypeStruct((bins, rows, de...  0.88 us

profile of v3, /device:TPU:0, one launch (start us, length us, event | category | flops | bytes accessed | tf_op | source)
XLA Modules:
  0.0 13.3 jit_solution(5800505235412770217)
XLA Ops:
  0.6 11.8 %shard_map.86 = (f32[20,8,8,90]{3,2,1,0:T(8,128)S(1)}, f32[8,2,360]{2,1,0:T(2,128)S(1)}) custom-call(f32[20,8,2,360]{3,2,1,0:T(2,128)} %q_hbm.1, f32[8,2,360]{2,1,0:T(2,128)} %mc_hbm.1, f32[8,2,360]{2,1,0:T(2,128)} %temp_hbm.1, f32[2]{0:T(128)} %span_hbm.1, f32[20]{0:T(128)} %fall_hbm.1, f32[8,8,90]{2,1,0:T(8,128)} %zc_hbm.1, f32[20,20]{1,0:T(8,128)} %rate_hbm.1), custom_call_target="tpu_custom_call" | custom-call | tf_op jit(solution)/shard_map/pallas_call | solution.py:472
  12.4 0.9 %shard_map.87 = (f32[20,8,8,90]{3,2,1,0:T(8,128)}, f32[8,2,360]{2,1,0:T(2,128)}) custom-call(f32[20,8,8,90]{3,2,1,0:T(8,128)S(1)} %get-tuple-element.4.dust_ref, f32[8,2,360]{2,1,0:T(2,128)S(1)} %get-tuple-element.5.height_ref), custom_call_target="tpu_custom_call" | custom-call | tf_op jit(solution)/shard_map/pallas_call | solution.py:500

commit v4 on v3

--- a/solution.py
+++ b/solution.py
@@ -51,13 +51,77 @@
     return [(r, r + 1) for r in range(1, rows - 1, 2)] + [(0, rows - 1)]
 
 
+def work_off(width, bins, levels, group, rows_at, packed, flow, ratio, dens, zonal, merge, store):
+    stack, body, rest = 2 * bins, bins // TILE * TILE, bins % TILE
+    padded = -(-stack // 16) * 16
+    piece = -(-(width + 2) // 3)
+    base_row, ends = 6 * TILE, slice(7 * TILE, 7 * TILE + TILE // 2)
+    lane = lax.broadcasted_iota(jnp.int32, (TILE, LANES), 1)
+    sub = lax.broadcasted_iota(jnp.int32, (TILE, LANES), 0)
+    near_end = (lane < piece - 1) | (lane == LANES - 1)
+    second = lane < 2 * piece - 1
+    upper = sub < TILE // 2
+
+    def back(x, p):
+        return pltpu.roll(x, (piece * p - width - 2) % LANES, 1)
+
+    def spread(pair):
+        a, b = pair
+        return jnp.concatenate([
+            jnp.broadcast_to(a, (body, LANES)), jnp.broadcast_to(b, (body, LANES)),
+            jnp.where(sub < rest, a, b)], 0)
+
+    unpacked = []
+    for read in packed:
+        y = read(slice(0, base_row))
+        x = [y[n * TILE : (n + 1) * TILE] for n in range(6)]
+        extra = [jnp.where(near_end, back(a, 0), jnp.where(second, back(b, 1), back(c, 2)))
+                 for a, b, c in (x[:3], x[3:])]
+        a, b = read(slice(base_row, base_row + TILE)), read(ends)
+        b = jnp.concatenate([b, b], 0)
+        outer = jnp.where(near_end, back(a, 0), back(b, 2))
+        inner = second & jnp.logical_not(near_end)
+        b = jnp.where(upper, b, jnp.where(inner, back(a, 1), pltpu.roll(outer, TILE // 2, 0)))
+        unpacked += [x[:4] + [a], x[4:] + extra + [b]]
+    moved = []
+    ks = range(group * levels, (group + len(packed)) * levels)
+    for n, k in enumerate(ks):
+        summed = jnp.concatenate(unpacked[n], 0) + flow
+        settled = ratio(k) * summed
+        flow = summed - settled
+        up, stay, down = (spread(pair) for pair in zonal(k))
+        moved.append(stay * settled + up * pltpu.roll(settled, 1, 1)
+                     - down * pltpu.roll(settled, LANES - 1, 1))
+    x = jnp.concatenate(moved, 1)
+    x = jnp.concatenate([x, jnp.zeros((padded - stack, x.shape[1]), jnp.float32)], 0)
+    high = x.astype(jnp.bfloat16)
+    low = (x - high.astype(jnp.float32)).astype(jnp.bfloat16)
+    coag = jnp.dot(merge[...], jnp.concatenate([high, low, high], 0), preferred_element_type=jnp.float32)
+    for n, k in enumerate(ks):
+        x = moved[n]
+        x = (x + spread(dens(k)) * x * coag[:stack, n * LANES : (n + 1) * LANES])[:, :width]
+        for side, at in enumerate(rows_at):
+            store[:body, at, k, :] = x[side * body : (side + 1) * body]
+            low_end = 2 * body + side * rest
+            store[body:, at, k, :] = x[low_end : low_end + rest]
+    return flow
+
+
+def read_rows(ref, r, r2, k):
+    return ref[r, k : k + 1], ref[r2, k : k + 1]
+
+
+def read_levels(ref, r, r2, k):
+    return ref[k, r : r + 1], ref[k, r2 : r2 + 1]
+
+
 def kernel(
     n_lat, n_lev,
     q_hbm, mc_hbm, temp_hbm, span_hbm, fall_hbm, zc_hbm, rate_hbm,
-    out_ref, height_ref,
+    out_ref, height_ref, pair_ref, flow_ref, late_ref, ratio_v, dens_v, z_v, stay_v, east_v, merge_v,
     q_v, mc_v, temp_v, span_s, fall_s, zc_v, rate_v,
     main_s, main_r, thick_s, thick_r, south_r, north_r, mcn_r, below_s, below_r,
-    halo_s, halo_r, adv_v, ratio_v, dens_v, full_v, z_v, merge_v,
+    halo_s, halo_r, adv_v, full_v,
     q_sem, load_sem, main_ss, main_rs, thick_ss, thick_rs,
     below_ss, below_rs, north_ss, north_rs, south_ss, south_rs, halo_sem,
 ):
@@ -343,49 +407,33 @@
     halo_copy.wait_recv()
     halo = halo_r[...]
     for r in range(rows):
-        z_v[r] = jnp.where(zlane == width, pltpu.roll(halo, width - r, 1), z_v[r])
+        z = jnp.where(zlane == width, pltpu.roll(halo, width - r, 1), z_v[r])
+        up, down = jnp.maximum(z, 0.0), jnp.minimum(z, 0.0)
+        z_v[r] = up
+        east_v[r] = pltpu.roll(down, LANES - 1, 1)
+        stay_v[r] = 1.0 + down - pltpu.roll(up, LANES - 1, 1)
 
     def collect(ch):
         r, r2 = pairs[ch]
         flow = jnp.zeros((stack, LANES), jnp.float32)
+        last = ch == len(pairs) - 1
         for group in range(0, n_lev, 2):
             for m in (group, group + 1):
                 @pl.when(j != m)
                 def _():
                     main_arrival(m, ch).wait_recv()
 
-            moved = []
-            ks = range(group * levels, (group + 2) * levels)
-            unpacked = []
-            for m in (group, group + 1):
-                x = tiles(main_r[m, ch, :base_row])
-                extra = [jnp.where(first, back(a, 0), jnp.where(second, back(b, 1), back(c, 2)))
-                         for a, b, c in (x[:3], x[3:])]
-                a, b = sixteen(main_r[m, ch, base_row : base_row + TILE], main_r[m, ch, ends])
-                unpacked += [x[:4] + [a], x[4:] + extra + [b]]
-            for k in ks:
-                summed = jnp.concatenate(unpacked[k - group * levels], 0) + flow
-                settled = ratio_v[ch, k] * summed
-                flow = summed - settled
-                z, z2 = z_v[r, k : k + 1], z_v[r2, k : k + 1]
-                up = spread(jnp.maximum(z, 0.0), jnp.maximum(z2, 0.0))
-                down = spread(jnp.minimum(z, 0.0), jnp.minimum(z2, 0.0))
-                west = up * pltpu.roll(settled, 1, 1) + down * settled
-                moved.append(settled + west - pltpu.roll(west, LANES - 1, 1))
-            x = jnp.concatenate(moved, 1)
-            x = jnp.concatenate([x, jnp.zeros((padded - stack, x.shape[1]), jnp.float32)], 0)
-            high = x.astype(jnp.bfloat16)
-            low = (x - high.astype(jnp.float32)).astype(jnp.bfloat16)
-            coag = jnp.dot(merge_v[...], jnp.concatenate([high, low, high], 0),
-                           preferred_element_type=jnp.float32)
-            for n, k in enumerate(ks):
-                dens = spread(dens_v[k, r : r + 1], dens_v[k, r2 : r2 + 1])
-                x = moved[n]
-                x = (x + dens * x * coag[:stack, n * LANES : (n + 1) * LANES])[:, :width]
-                out_ref[:body, r, k, :] = x[:body]
-                out_ref[:body, r2, k, :] = x[body : 2 * body]
-                out_ref[body:, r, k, :] = x[2 * body : 2 * body + rest]
-                out_ref[body:, r2, k, :] = x[2 * body + rest :]
+            if last and group == n_lev - 2:
+                flow_ref[...] = flow
+                for m in (group, group + 1):
+                    late_ref[m - group] = main_r[m, ch]
+            else:
+                flow = work_off(
+                    width, bins, levels, group, (0, 1) if last else (r, r2),
+                    [lambda at, m=m: main_r[m, ch, at] for m in (group, group + 1)], flow,
+                    lambda k: ratio_v[ch, k], lambda k: read_levels(dens_v, r, r2, k),
+                    lambda k: [read_rows(ref, r, r2, k) for ref in (z_v, stay_v, east_v)],
+                    merge_v, pair_ref if last else out_ref)
 
     for ch in range(final):
         collect(ch)
@@ -431,16 +479,26 @@
         main_copy(m, final).wait_send()
 
 
-def hand_over(dust_ref, height_ref, dust_out, height_out, sem_out):
-    pieces = sem_out.shape[0] - 1
-    step = dust_ref.shape[0] // pieces
-    leave = []
-    for p in range(pieces):
-        part = pl.ds(p * step, step)
-        leave.append(pltpu.make_async_copy(dust_ref.at[part], dust_out.at[part], sem_out.at[p]))
-    leave.append(pltpu.make_async_copy(height_ref, height_out, sem_out.at[pieces]))
+def hand_over(
+    n_lev, dust_ref, height_ref, pair_ref, flow_ref, late_ref, ratio_v, dens_v, z_v, stay_v, east_v, merge_v,
+    dust_out, height_out, pair_v, sem_out,
+):
+    bins, rows, deep, width = dust_ref.shape
+    pairs = row_pairs(rows)
+    leave = [pltpu.make_async_copy(dust_ref.at[:, 1 : rows - 1], dust_out.at[:, 1 : rows - 1], sem_out.at[0]),
+             pltpu.make_async_copy(height_ref, height_out, sem_out.at[1])]
     for copy in leave:
         copy.start()
+    r, r2 = pairs[-1]
+    pair_v[...] = pair_ref[...]
+    work_off(
+        width, bins, deep // n_lev, n_lev - 2, (0, 1),
+        [lambda at, m=m: late_ref[m, at] for m in range(2)], flow_ref[...],
+        lambda k: ratio_v[len(pairs) - 1, k], lambda k: read_levels(dens_v, r, r2, k),
+        lambda k: [read_rows(ref, r, r2, k) for ref in (z_v, stay_v, east_v)], merge_v, pair_v)
+    for side, at in enumerate((r, r2)):
+        leave.append(pltpu.make_async_copy(pair_v.at[:, side], dust_out.at[:, at], sem_out.at[2 + side]))
+        leave[-1].start()
     for copy in leave:
         copy.wait()
 
@@ -469,14 +527,23 @@
         halo = pltpu.VMEM((deep, LANES), f32)
         dma = pltpu.SemaphoreType.DMA
         args = [pltpu.with_memory_space_constraint(x, pltpu.HBM) for x in args]
-        dust, height = pl.pallas_call(
+        outcome = pl.pallas_call(
             functools.partial(kernel, n_lat, n_lev),
             out_shape=(
                 pltpu.VMEM((bins, rows, deep, width), f32),
                 pltpu.VMEM((rows, levels, total), f32),
+                pltpu.VMEM((bins, 2, deep, width), f32),
+                pltpu.VMEM((stack, LANES), f32),
+                pltpu.VMEM((2, 7 * TILE + TILE // 2, LANES), f32),
+                pltpu.VMEM((chunks, deep, stack, LANES), f32),
+                pltpu.VMEM((deep, rows, LANES), f32),
+                pltpu.VMEM((rows, deep, LANES), f32),
+                pltpu.VMEM((rows, deep, LANES), f32),
+                pltpu.VMEM((rows, deep, LANES), f32),
+                pltpu.VMEM((padded, 3 * padded), jnp.bfloat16),
             ),
             in_specs=[hbm] * 7,
-            out_specs=(vmem, vmem),
+            out_specs=(vmem,) * 11,
             scratch_shapes=[
                 pltpu.VMEM((rows, levels, bins, total), f32),
                 pltpu.VMEM((rows, levels, total), f32), pltpu.VMEM((rows, levels, total), f32),
@@ -485,10 +552,7 @@
                 main, main, thick, thick, edge, edge, pltpu.VMEM((levels, total), f32), tile, tile,
                 halo, halo,
                 pltpu.VMEM((chunks, levels, count, stack, LANES), f32),
-                pltpu.VMEM((chunks, deep, stack, LANES), f32),
-                pltpu.VMEM((deep, rows, LANES), f32), pltpu.VMEM((deep, rows, LANES), f32),
-                pltpu.VMEM((rows, deep, LANES), f32),
-                                pltpu.VMEM((padded, 3 * padded), jnp.bfloat16),
+                pltpu.VMEM((deep, rows, LANES), f32),
                 dma((rows * levels,)), dma((6,)),
                 dma((n_lev, chunks)), dma((n_lev, chunks)),
                 dma((n_lev,)), dma((n_lev,)), dma((n_lev,)), dma((n_lev,)),
@@ -498,15 +562,15 @@
                 collective_id=0, has_side_effects=True, vmem_limit_bytes=32 * 1024 * 1024),
         )(*args)
         return pl.pallas_call(
-            hand_over,
+            functools.partial(hand_over, n_lev),
             out_shape=(
                 jax.ShapeDtypeStruct((bins, rows, deep, width), f32),
-                jax.ShapeDtypeStruct(height.shape, f32)),
-            in_specs=[vmem, vmem],
+                jax.ShapeDtypeStruct((rows, levels, total), f32)),
+            in_specs=[vmem] * 11,
             out_specs=(hbm, hbm),
-            scratch_shapes=[dma((5,))],
+            scratch_shapes=[pltpu.VMEM((bins, 2, deep, width), f32), dma((4,))],
             compiler_params=pltpu.CompilerParams(vmem_limit_bytes=32 * 1024 * 1024),
-        )(dust, height)
+        )(*outcome)
 
     in_specs = (
         P(None, "lat", "lev", None),

time: 13.5 us -> 13.3 us (0.985)
  Pallas kernels: 12.6 us -> 12.4 us
    pallas_call x1, Pallas kernels: 11.8 us -> 11.4 us  [on_device(): pl.pallas_call(functools.partial(kernel, n_lat, n_lev), out_shape=(pltpu....]
    pallas_call x1, Pallas kernels: 0.88 us -> 1.05 us  [on_device(): pl.pallas_call(functools.partial(hand_over, n_lev), out_shape=(jax.ShapeD...]
where the time goes in v4:
time: 13.3 us; the launch traced here: 13.1 us
  Pallas kernels  12.4 us (93%)
  between operations  0.64 us (5%)
    pallas_call x1, Pallas kernels, on_device(): pl.pallas_call(functools.partial(kernel, n_lat, n_lev), out_shape=(pltpu....  11.4 us
    pallas_call x1, Pallas kernels, on_device(): pl.pallas_call(functools.partial(hand_over, n_lev), out_shape=(jax.ShapeD...  1.05 us

profile of v4, /device:TPU:0, one launch (start us, length us, event | category | flops | bytes accessed | tf_op | source)
XLA Modules:
  0.0 13.1 jit_solution(99696431995800099)
XLA Ops:
  0.6 11.4 %shard_map.86 = (f32[20,8,8,90]{3,2,1,0:T(8,128)S(1)}, f32[8,2,360]{2,1,0:T(2,128)S(1)}, f32[20,2,8,90]{3,2,1,0:T(8,128)S(1)}, f32[40,128]{1,0:T(8,128)S(1)}, f3...) custom-call(f32[20,8,2,360]{3,2,1,0:T(2,128)} %q_hbm.1, ...), custom_call_target="tpu_custom_call" | custom-call | tf_op jit(solution)/shard_map/pallas_call | solution.py:530
  12.0 1.1 %shard_map.87 = (f32[20,8,8,90]{3,2,1,0:T(8,128)}, f32[8,2,360]{2,1,0:T(2,128)}) custom-call(f32[20,8,8,90]{3,2,1,0:T(8,128)S(1)} %get-tuple-element.13.dust_ref, f32[8,2,360]{2,1,0:T(2,128)S(1)} %get-tuple-element.14.height_ref, f32[20,2,8,90]{3,2,1,0:T(8,128)S(1)} %get-tuple-element.15.pair_ref, f32[40,128]{1,0:T(8,128)S(1)} %get-tuple-element.16.flow_ref, ...), custom_call_target="tpu_custom_call" | custom-call | tf_op jit(solution)/shard_map/pallas_call | solution.py:564

commit v5 on v4

--- a/solution.py
+++ b/solution.py
@@ -334,84 +334,60 @@
         below_copy(m).start()
     below_r[pl.ds(j, 1)] = below_s[pl.ds(j, 1)]
 
-    for load in small[4:]:
-        load.wait()
-    rate = rate_v[...]
-    r0 = lax.broadcasted_iota(jnp.int32, rate.shape, 0)
-    r1 = lax.broadcasted_iota(jnp.int32, rate.shape, 1)
-    merging = jnp.where(r1 < r0, rate, jnp.where(r1 > r0, -rate, 0.0))
-
-    def place(n):
-        tail = n - 2 * body
-        side = jnp.where(n < 2 * body, n // body, tail // rest)
-        kind = jnp.where(n < 2 * body, n - side * body, body + tail - side * rest)
-        return side, jnp.where(n < stack, kind, -1)
-
-    _, kind = place(lax.broadcasted_iota(jnp.int32, (padded, bins), 0))
-    pick = jnp.where(kind == lax.broadcasted_iota(jnp.int32, (padded, bins), 1), 1.0, 0.0)
-    both = jnp.dot(pick, merging, precision=HIGHEST, preferred_element_type=jnp.float32)
-    both = lax.dot_general(both, pick, (((1,), (1,)), ((), ())), precision=HIGHEST,
-                           preferred_element_type=jnp.float32)
-    side0, _ = place(lax.broadcasted_iota(jnp.int32, (padded, padded), 0))
-    side1, _ = place(lax.broadcasted_iota(jnp.int32, (padded, padded), 1))
-    both = jnp.where(side0 == side1, both, 0.0)
-    high = both.astype(jnp.bfloat16)
-    low = (both - high.astype(jnp.float32)).astype(jnp.bfloat16)
-    merge_v[...] = jnp.concatenate([high, high, low], 1)
-
-    def column(first, n):
-        x = jnp.zeros((TILE, LANES), jnp.float32)
-        for s in range(TILE):
-            x = jnp.where(sub == s, fall_s[first + s % n], x)
-        return x
-
-    fall = [column(f * TILE, TILE) for f in range(full)]
-    fall = jnp.concatenate(fall + fall + [column(body, rest)], 0)
-
     def spread(a, b):
         return jnp.concatenate([
             jnp.broadcast_to(a, (body, LANES)), jnp.broadcast_to(b, (body, LANES)),
             jnp.where(sub < rest, a, b)], 0)
 
-    @pl.when(jnp.logical_not(has_south))
-    def _():
-        south_r[...] = jnp.zeros_like(south_r)
-
-    @pl.when(jnp.logical_not(has_north))
-    def _():
-        north_r[...] = jnp.zeros_like(north_r)
-        mcn_r[...] = jnp.zeros_like(mcn_r)
-
-    @pl.when(has_south)
-    def _():
-        for k in range(levels):
-            pltpu.make_async_remote_copy(
-                q_hbm.at[:, 0, k, :], south_r.at[k], north_ss.at[k], north_rs.at[k], (i - 1, j), MESH).wait_recv()
-
-    @pl.when(has_north)
-    def _():
-        for k in range(levels):
-            pltpu.make_async_remote_copy(
-                q_hbm.at[:, 0, k, :], north_r.at[k], south_ss.at[k], south_rs.at[k], (i + 1, j), MESH).wait_recv()
-        pltpu.make_async_remote_copy(
-            mc_hbm.at[0], mcn_r, south_ss.at[levels], south_rs.at[levels], (i + 1, j), MESH).wait_recv()
-
-    final = len(pairs) - 1
-    prepare(final)
-    send(final)
-    for ch, (r, r2) in enumerate(pairs):
-        for k in range(deep):
-            t = spread(full_v[k, r : r + 1], full_v[k, r2 : r2 + 1])
-            ratio_v[ch, k] = t / (t + fall)
-
-    halo_copy.wait_recv()
-    halo = halo_r[...]
-    for r in range(rows):
-        z = jnp.where(zlane == width, pltpu.roll(halo, width - r, 1), z_v[r])
-        up, down = jnp.maximum(z, 0.0), jnp.minimum(z, 0.0)
-        z_v[r] = up
-        east_v[r] = pltpu.roll(down, LANES - 1, 1)
-        stay_v[r] = 1.0 + down - pltpu.roll(up, LANES - 1, 1)
+    def ready():
+        for load in small[4:]:
+            load.wait()
+        rate = rate_v[...]
+        r0 = lax.broadcasted_iota(jnp.int32, rate.shape, 0)
+        r1 = lax.broadcasted_iota(jnp.int32, rate.shape, 1)
+        merging = jnp.where(r1 < r0, rate, jnp.where(r1 > r0, -rate, 0.0))
+
+        def place(n):
+            tail = n - 2 * body
+            side = jnp.where(n < 2 * body, n // body, tail // rest)
+            kind = jnp.where(n < 2 * body, n - side * body, body + tail - side * rest)
+            return side, jnp.where(n < stack, kind, -1)
+
+        _, kind = place(lax.broadcasted_iota(jnp.int32, (padded, bins), 0))
+        pick = jnp.where(kind == lax.broadcasted_iota(jnp.int32, (padded, bins), 1), 1.0, 0.0)
+        both = jnp.dot(pick, merging, precision=HIGHEST, preferred_element_type=jnp.float32)
+        both = lax.dot_general(both, pick, (((1,), (1,)), ((), ())), precision=HIGHEST,
+                               preferred_element_type=jnp.float32)
+        side0, _ = place(lax.broadcasted_iota(jnp.int32, (padded, padded), 0))
+        side1, _ = place(lax.broadcasted_iota(jnp.int32, (padded, padded), 1))
+        both = jnp.where(side0 == side1, both, 0.0)
+        high = both.astype(jnp.bfloat16)
+        low = (both - high.astype(jnp.float32)).astype(jnp.bfloat16)
+        merge_v[...] = jnp.concatenate([high, high, low], 1)
+
+        def column(first, n):
+            x = jnp.zeros((TILE, LANES), jnp.float32)
+            for s in range(TILE):
+                x = jnp.where(sub == s, fall_s[first + s % n], x)
+            return x
+
+        fall = [column(f * TILE, TILE) for f in range(full)]
+        fall = jnp.concatenate(fall + fall + [column(body, rest)], 0)
+
+        for ch, (r, r2) in enumerate(pairs):
+            for k in range(deep):
+                t = spread(full_v[k, r : r + 1], full_v[k, r2 : r2 + 1])
+                ratio_v[ch, k] = t / (t + fall)
+
+        halo_copy.wait_recv()
+        halo = halo_r[...]
+        for r in range(rows):
+            z = jnp.where(zlane == width, pltpu.roll(halo, width - r, 1), z_v[r])
+            up, down = jnp.maximum(z, 0.0), jnp.minimum(z, 0.0)
+            z_v[r] = up
+            east_v[r] = pltpu.roll(down, LANES - 1, 1)
+            stay_v[r] = 1.0 + down - pltpu.roll(up, LANES - 1, 1)
+
 
     def collect(ch):
         r, r2 = pairs[ch]
@@ -435,7 +411,44 @@
                     lambda k: [read_rows(ref, r, r2, k) for ref in (z_v, stay_v, east_v)],
                     merge_v, pair_ref if last else out_ref)
 
-    for ch in range(final):
+    @pl.when(j < half_way)
+    def _():
+        ready()
+        collect(0)
+
+    @pl.when(jnp.logical_not(has_south))
+    def _():
+        south_r[...] = jnp.zeros_like(south_r)
+
+    @pl.when(jnp.logical_not(has_north))
+    def _():
+        north_r[...] = jnp.zeros_like(north_r)
+        mcn_r[...] = jnp.zeros_like(mcn_r)
+
+    @pl.when(has_south)
+    def _():
+        for k in range(levels):
+            pltpu.make_async_remote_copy(
+                q_hbm.at[:, 0, k, :], south_r.at[k], north_ss.at[k], north_rs.at[k], (i - 1, j), MESH).wait_recv()
+
+    @pl.when(has_north)
+    def _():
+        for k in range(levels):
+            pltpu.make_async_remote_copy(
+                q_hbm.at[:, 0, k, :], north_r.at[k], south_ss.at[k], south_rs.at[k], (i + 1, j), MESH).wait_recv()
+        pltpu.make_async_remote_copy(
+            mc_hbm.at[0], mcn_r, south_ss.at[levels], south_rs.at[levels], (i + 1, j), MESH).wait_recv()
+
+    final = len(pairs) - 1
+    prepare(final)
+    send(final)
+
+    @pl.when(j >= half_way)
+    def _():
+        ready()
+        collect(0)
+
+    for ch in range(1, final):
         collect(ch)
 
     for m in range(n_lev):
@@ -487,17 +500,21 @@
     pairs = row_pairs(rows)
     leave = [pltpu.make_async_copy(dust_ref.at[:, 1 : rows - 1], dust_out.at[:, 1 : rows - 1], sem_out.at[0]),
              pltpu.make_async_copy(height_ref, height_out, sem_out.at[1])]
+    r, r2 = pairs[-1]
+    done = deep - 2 * (deep // n_lev)
+    for side, at in enumerate((r, r2)):
+        leave.append(pltpu.make_async_copy(
+            pair_ref.at[:, side, :done], dust_out.at[:, at, :done], sem_out.at[4 + side]))
     for copy in leave:
         copy.start()
-    r, r2 = pairs[-1]
-    pair_v[...] = pair_ref[...]
     work_off(
         width, bins, deep // n_lev, n_lev - 2, (0, 1),
         [lambda at, m=m: late_ref[m, at] for m in range(2)], flow_ref[...],
         lambda k: ratio_v[len(pairs) - 1, k], lambda k: read_levels(dens_v, r, r2, k),
         lambda k: [read_rows(ref, r, r2, k) for ref in (z_v, stay_v, east_v)], merge_v, pair_v)
     for side, at in enumerate((r, r2)):
-        leave.append(pltpu.make_async_copy(pair_v.at[:, side], dust_out.at[:, at], sem_out.at[2 + side]))
+        leave.append(pltpu.make_async_copy(
+            pair_v.at[:, side, done:], dust_out.at[:, at, done:], sem_out.at[2 + side]))
         leave[-1].start()
     for copy in leave:
         copy.wait()
@@ -568,7 +585,7 @@
                 jax.ShapeDtypeStruct((rows, levels, total), f32)),
             in_specs=[vmem] * 11,
             out_specs=(hbm, hbm),
-            scratch_shapes=[pltpu.VMEM((bins, 2, deep, width), f32), dma((4,))],
+            scratch_shapes=[pltpu.VMEM((bins, 2, deep, width), f32), dma((6,))],
             compiler_params=pltpu.CompilerParams(vmem_limit_bytes=32 * 1024 * 1024),
         )(*outcome)
 

time: 13.3 us -> 13.2 us (level)
  no operation moved by 1% of the time
where the time goes in v5:
time: 13.2 us; the launch traced here: 13 us
  Pallas kernels  12.4 us (94%)
  between operations  0.64 us (5%)
    pallas_call x1, Pallas kernels, on_device(): pl.pallas_call(functools.partial(kernel, n_lat, n_lev), out_shape=(pltpu....  11.4 us
    pallas_call x1, Pallas kernels, on_device(): pl.pallas_call(functools.partial(hand_over, n_lev), out_shape=(jax.ShapeD...  1.03 us

profile of v5, /device:TPU:0, one launch (start us, length us, event | category | flops | bytes accessed | tf_op | source)
XLA Modules:
  0.0 13.0 jit_solution(16363329864831970984)
XLA Ops:
  0.6 11.4 %shard_map.86 = (f32[20,8,8,90]{3,2,1,0:T(8,128)S(1)}, f32[8,2,360]{2,1,0:T(2,128)S(1)}, f32[20,2,8,90]{3,2,1,0:T(8,128)S(1)}, f32[40,128]{1,0:T(8,128)S(1)}, f3...) custom-call(f32[20,8,2,360]{3,2,1,0:T(2,128)} %q_hbm.1, ...), custom_call_target="tpu_custom_call" | custom-call | tf_op jit(solution)/shard_map/pallas_call | solution.py:547
  12.0 1.0 %shard_map.87 = (f32[20,8,8,90]{3,2,1,0:T(8,128)}, f32[8,2,360]{2,1,0:T(2,128)}) custom-call(f32[20,8,8,90]{3,2,1,0:T(8,128)S(1)} %get-tuple-element.13.dust_ref, f32[8,2,360]{2,1,0:T(2,128)S(1)} %get-tuple-element.14.height_ref, f32[20,2,8,90]{3,2,1,0:T(8,128)S(1)} %get-tuple-element.15.pair_ref, f32[40,128]{1,0:T(8,128)S(1)} %get-tuple-element.16.flow_ref, ...), custom_call_target="tpu_custom_call" | custom-call | tf_op jit(solution)/shard_map/pallas_call | solution.py:581

commit v6 on v4

--- a/solution.py
+++ b/solution.py
@@ -289,8 +289,9 @@
         for copy in south_copies:
             copy.start()
 
-    for m in far:
+    for m in far + near:
         thick_copy(m).start()
+    halo_copy.start()
     for m in far:
         main_copy(m, 0).start()
 
@@ -299,9 +300,6 @@
         for copy in north_copies:
             copy.start()
 
-    halo_copy.start()
-    for m in near:
-        thick_copy(m).start()
     for m in near:
         main_copy(m, 0).start()
     main_r[pl.ds(j, 1), 0] = main_s[pl.ds(j, 1), 0]

time: 13.3 us -> 13.3 us (level)
  no operation moved by 1% of the time
where the time goes in v6:
time: 13.3 us; the launch traced here: 13.1 us
  Pallas kernels  12.4 us (93%)
  between operations  0.64 us (5%)
    pallas_call x1, Pallas kernels, on_device(): pl.pallas_call(functools.partial(kernel, n_lat, n_lev), out_shape=(pltpu....  11.4 us
    pallas_call x1, Pallas kernels, on_device(): pl.pallas_call(functools.partial(hand_over, n_lev), out_shape=(jax.ShapeD...  1.05 us

profile of v6, /device:TPU:0, one launch (start us, length us, event | category | flops | bytes accessed | tf_op | source)
XLA Modules:
  0.0 13.1 jit_solution(6665000396223950766)
XLA Ops:
  0.6 11.4 %shard_map.86 = (f32[20,8,8,90]{3,2,1,0:T(8,128)S(1)}, f32[8,2,360]{2,1,0:T(2,128)S(1)}, f32[20,2,8,90]{3,2,1,0:T(8,128)S(1)}, f32[40,128]{1,0:T(8,128)S(1)}, f3...) custom-call(f32[20,8,2,360]{3,2,1,0:T(2,128)} %q_hbm.1, ...), custom_call_target="tpu_custom_call" | custom-call | tf_op jit(solution)/shard_map/pallas_call | solution.py:528
  12.0 1.1 %shard_map.87 = (f32[20,8,8,90]{3,2,1,0:T(8,128)}, f32[8,2,360]{2,1,0:T(2,128)}) custom-call(f32[20,8,8,90]{3,2,1,0:T(8,128)S(1)} %get-tuple-element.13.dust_ref, f32[8,2,360]{2,1,0:T(2,128)S(1)} %get-tuple-element.14.height_ref, f32[20,2,8,90]{3,2,1,0:T(8,128)S(1)} %get-tuple-element.15.pair_ref, f32[40,128]{1,0:T(8,128)S(1)} %get-tuple-element.16.flow_ref, ...), custom_call_target="tpu_custom_call" | custom-call | tf_op jit(solution)/shard_map/pallas_call | solution.py:562
